TPU v7x, 128 devices: a whole 4x4x4 slice. The times are simulated.
128 devices in a mesh: team: 8 (over y_lo, z), rep: 16 (over x, y_hi, core).
Axes of the slice: x: 4, y: 4 (y_hi: 2, y_lo: 2; y = y_hi * 2 + y_lo), z: 4, core: 2. Of those that a mesh axis runs over, the one named last changes fastest.
Arguments:
- affinity: bfloat16 [8, 256, 8, 128, 128], P('team', 'rep'), as said below
- col_index: int32 [8, 256, 8], P('team', 'rep'), may hold values from 0 to 31, all different within a row
- labels: int32 [32768], P(('rep', 'team')), may hold values from 0 to 511
Outputs:
- diffused: bfloat16 [32768, 512], P(('rep', 'team'))
Inputs may be any that keep to these rules, and one draw needn't show every extreme that they name: `affinity`: every entry is positive. `col_index`: the 8 block columns of one block row are different.
All inputs are finite; a program needn't handle non-finite values.
Results may differ from a plain program's by a relative error of at most 0.017.
Values may be sent and summed in bfloat16 or wider, within the bound.
A program may use at most 128 MiB of HBM per device.

v0:
```python
import jax
import jax.numpy as jnp
from jax import lax
from jax.sharding import PartitionSpec as P

C = 512
ITERS = 3


def on_device(affinity, col_index, labels):
    panels = affinity[0]
    columns = col_index[0]
    block = panels.shape[-1]
    slots = panels.shape[1]
    rows_here = labels.shape[0]
    classes = jnp.arange(C, dtype=jnp.int32)
    seeded = (labels[:, None] == classes[None, :]).astype(jnp.float32) * 16.0
    current = seeded.astype(jnp.bfloat16)
    for step_index in range(ITERS):
        gathered = lax.all_gather(current, "rep", axis=0, tiled=True).reshape(-1, block, C)
        block_count = lax.axis_size("team") * rows_here // block
        summed = jnp.zeros((block_count, block, C), jnp.float32)
        for slot_index in range(slots):
            picked = gathered[columns[:, slot_index]]
            summed = summed + jnp.einsum(
                "iab,ibc->iac", panels[:, slot_index], picked, preferred_element_type=jnp.float32
            )
        summed_all = lax.psum_scatter(
            summed.reshape(lax.axis_size("team") * rows_here, C).astype(jnp.bfloat16),
            "team",
            scatter_dimension=0,
            tiled=True,
        ).astype(jnp.float32)
        blended = 0.9 * summed_all + 0.1 * seeded
        scale_rows = lax.rsqrt(jnp.mean(blended * blended, axis=-1, keepdims=True) + 1e-06)
        current = (blended * scale_rows).astype(jnp.bfloat16)
    return current


def solution(mesh):
    in_specs = (P("team", "rep", None, None, None), P("team", "rep", None), P(("rep", "team")))
    out_specs = P(("rep", "team"), None)
    return jax.shard_map(
        on_device, mesh=mesh, in_specs=in_specs, out_specs=out_specs, check_vma=False
    )
```

profile of v0, /device:TPU:0, one launch (start us, length us, event | category | flops | bytes accessed | tf_op | source)
XLA Modules:
  0.0 504.4 jit_solution(15811978290454994971)
XLA Ops:
  6.5 1.5 select_convert_fusion
  8.1 4.7 copy.6
  12.9 55.3 %all-gather.4.cloned.1.call-done = bf16[4096,512]{1,0:T(8,128)(2,1)} async-done(((bf16[256,512]{1,0:T(8,128)(2,1)}), bf16[4096,512]{1,0:T(8,128)(2,1)}) %all-gather.4.cloned.1.call-update) | async-done | bytes 4194320 | tf_op jit(solution)/shard_map/all_gather | solution.py:20
  68.2 2.9 gather_fusion.7
  71.1 4.2 gather_fusion.6
  75.3 4.2 gather_fusion.5
  79.5 4.2 gather_fusion.4
  83.7 4.3 gather_fusion.3
  87.9 4.2 gather_fusion.2
  92.1 4.2 gather_fusion.1
  96.3 4.2 gather_fusion
  100.5 2.6 fusion.21
  104.2 0.7 fusion.18
  104.9 0.9 copy-done.13
  105.8 2.7 fusion.15
  108.5 2.7 fusion.12
  111.2 2.6 fusion.9
  113.8 2.6 fusion.6
  116.5 2.7 fusion.3
  119.2 10.8 %add_convert_fusion.2 = bf16[16,512,128]{1,2,0:T(8,128)(2,1)} fusion(f32[16,512,128]{1,2,0:T(8,128)S(1)} %fusion.21, f32[16,512,128]{1,2,0:T(8,128)S(1)} %fusion.18, f32[16,512,128]{1,2,0:T(8,128)} %fusion.15, f32[16,512,128]{1,2,0:T(8,128)} %fusion.12, f32[16,512,128]{1,2,0:T(8,128)} %fusion.9, f32[16,512,128]{1,2,0:T(8,128)} %fusion.3, ...), kind=kOutput, calls=%fused_computation.27 | convolution fusion | flops 276824064 | bytes 34078720 | tf_op jit(solution)/shard_map/iab,ibc->iac/dot_general | solution.py:25
  130.1 41.6 %reduce-scatter.4.cloned.1.call-done = bf16[256,512]{1,0:T(8,128)(2,1)} async-done(((bf16[2048,512]{1,0:T(8,128)(2,1)}), bf16[256,512]{1,0:T(8,128)(2,1)}) %reduce-scatter.4.cloned.1.call-update) | async-done | bytes 262160 | tf_op jit(solution)/shard_map/reduce_scatter | solution.py:28
  171.7 1.2 multiply_reduce_fusion.2
  173.0 1.9 multiply_convert_fusion.2
  175.1 54.6 %all-gather.6.cloned.1.call-done = bf16[4096,512]{1,0:T(8,128)(2,1)} async-done(((bf16[256,512]{1,0:T(8,128)(2,1)}), bf16[4096,512]{1,0:T(8,128)(2,1)}) %all-gather.6.cloned.1.call-update) | async-done | bytes 4194320 | tf_op jit(solution)/shard_map/all_gather | solution.py:20
  229.7 2.9 gather_fusion.15
  232.6 4.2 gather_fusion.14
  236.8 4.3 gather_fusion.13
  241.0 4.2 gather_fusion.12
  245.2 4.2 gather_fusion.11
  249.4 4.2 gather_fusion.10
  253.6 4.2 gather_fusion.9
  257.8 4.2 gather_fusion.8
  262.0 2.6 fusion.22
  265.7 0.7 fusion.19
  266.3 0.9 copy-done.18
  267.2 2.7 fusion.16
  270.0 2.7 fusion.13
  272.7 2.6 fusion.10
  275.3 2.6 fusion.4
  277.9 2.7 fusion.7
  280.7 10.8 %add_convert_fusion.1 = bf16[16,512,128]{1,2,0:T(8,128)(2,1)} fusion(f32[16,512,128]{1,2,0:T(8,128)S(1)} %fusion.22, f32[16,512,128]{1,2,0:T(8,128)S(1)} %fusion.19, f32[16,512,128]{1,2,0:T(8,128)} %fusion.16, f32[16,512,128]{1,2,0:T(8,128)} %fusion.13, f32[16,512,128]{1,2,0:T(8,128)} %fusion.10, f32[16,512,128]{1,2,0:T(8,128)} %fusion.4, ...), kind=kOutput, calls=%fused_computation.26 | convolution fusion | flops 276824064 | bytes 34078720 | tf_op jit(solution)/shard_map/iab,ibc->iac/dot_general | solution.py:25
  291.6 41.8 %reduce-scatter.6.cloned.1.call-done = bf16[256,512]{1,0:T(8,128)(2,1)} async-done(((bf16[2048,512]{1,0:T(8,128)(2,1)}), bf16[256,512]{1,0:T(8,128)(2,1)}) %reduce-scatter.6.cloned.1.call-update) | async-done | bytes 262160 | tf_op jit(solution)/shard_map/reduce_scatter | solution.py:28
  333.4 1.2 multiply_reduce_fusion.1
  334.6 1.9 multiply_convert_fusion.1
  336.7 54.3 %all-gather.8.cloned.1.call-done = bf16[4096,512]{1,0:T(8,128)(2,1)} async-done(((bf16[256,512]{1,0:T(8,128)(2,1)}), bf16[4096,512]{1,0:T(8,128)(2,1)}) %all-gather.8.cloned.1.call-update) | async-done | bytes 4194320 | tf_op jit(solution)/shard_map/all_gather | solution.py:20
  391.1 2.9 gather_fusion.23
  393.9 4.2 gather_fusion.22
  398.1 4.2 gather_fusion.21
  402.3 4.2 gather_fusion.20
  406.5 4.3 gather_fusion.19
  410.7 4.2 gather_fusion.18
  415.0 4.2 gather_fusion.17
  419.1 4.2 gather_fusion.16
  423.4 2.6 fusion.5
  427.7 0.9 copy-done.17
  428.6 2.6 fusion.11
  431.2 2.7 fusion.14
  434.0 2.7 fusion.17
  436.7 2.6 fusion.20
  439.3 2.6 fusion.23
  441.9 10.7 %add_convert_fusion = bf16[16,512,128]{1,2,0:T(8,128)(2,1)} fusion(f32[16,512,128]{1,2,0:T(8,128)} %fusion.23, f32[16,512,128]{1,2,0:T(8,128)} %fusion.20, f32[16,512,128]{1,2,0:T(8,128)} %fusion.17, f32[16,512,128]{1,2,0:T(8,128)} %fusion.14, f32[16,512,128]{1,2,0:T(8,128)} %fusion.11, f32[16,512,128]{1,2,0:T(8,128)S(1)} %fusion.5, ...), kind=kOutput, calls=%fused_computation.25 | convolution fusion | flops 276824064 | bytes 34078720 | tf_op jit(solution)/shard_map/iab,ibc->iac/dot_general | solution.py:25
  452.6 41.8 %reduce-scatter.8.cloned.1.call-done = bf16[256,512]{1,0:T(8,128)(2,1)} async-done(((bf16[2048,512]{1,0:T(8,128)(2,1)}), bf16[256,512]{1,0:T(8,128)(2,1)}) %reduce-scatter.8.cloned.1.call-update) | async-done | bytes 262160 | tf_op jit(solution)/shard_map/reduce_scatter | solution.py:28
  494.5 1.2 multiply_reduce_fusion
  495.7 1.9 multiply_convert_fusion
  (64 shorter events, 4.7 us)
Async XLA Ops:
  6.5 61.7 %all-gather.4.cloned.1.call-start = ((), (), s32[]{:S(2)}) async-start(), calls=%async_computation.3 | async-start | bytes 4456448 | tf_op jit(solution)/shard_map/all_gather | solution.py:20
  8.1 4.8 copy-start.22
  8.1 163.6 %reduce-scatter.4.cloned.1.call-start = ((), (), s32[]{:S(2)}) async-start(), calls=%async_computation.4 | async-start | bytes 2359296 | tf_op jit(solution)/shard_map/reduce_scatter | solution.py:28
  100.5 3.0 copy-start
  100.5 3.7 copy-start.12
  104.2 1.6 copy-start.13
  105.8 2.7 copy-start.10
  108.5 2.7 copy-start.11
  111.2 2.6 copy-start.8
  113.8 2.6 copy-start.9
  130.0 41.7 %copy-start.21 = (s32[256]{0:T(256)S(1)}, s32[256]{0:T(256)}, u32[]{:S(2)}) copy-start(s32[256]{0:T(256)} %param.5) | copy-start | bytes 3076
  130.0 99.7 %all-gather.6.cloned.1.call-start = ((), (), s32[]{:S(2)}) async-start(), calls=%async_computation.5 | async-start | bytes 4456448 | tf_op jit(solution)/shard_map/all_gather | solution.py:20
  174.8 158.5 %reduce-scatter.6.cloned.1.call-start = ((), (), s32[]{:S(2)}) async-start(), calls=%async_computation.6 | async-start | bytes 2359296 | tf_op jit(solution)/shard_map/reduce_scatter | solution.py:28
  262.0 3.0 copy-start.1
  262.0 3.7 copy-start.19
  265.7 1.6 copy-start.18
  267.2 2.7 copy-start.16
  270.0 2.7 copy-start.14
  272.7 2.6 copy-start.15
  275.3 2.6 copy-start.6
  291.5 99.5 %all-gather.8.cloned.1.call-start = ((), (), s32[]{:S(2)}) async-start(), calls=%async_computation.7 | async-start | bytes 4456448 | tf_op jit(solution)/shard_map/all_gather | solution.py:20
  336.5 158.0 %reduce-scatter.8.cloned.1.call-start = ((), (), s32[]{:S(2)}) async-start(), calls=%async_computation.8 | async-start | bytes 2359296 | tf_op jit(solution)/shard_map/reduce_scatter | solution.py:28
  423.3 3.0 copy-start.2
  423.4 3.7 copy-start.20
  427.0 1.6 copy-start.17
  428.6 2.6 copy-start.7
  431.2 2.7 copy-start.5
  434.0 2.7 copy-start.4
  436.7 2.6 copy-start.3
Sparse Core Ops, SparseCore 0:
  9.8 58.4 all-gather.3
  130.2 41.5 reduce-scatter.3
  175.0 54.6 all-gather.5
  291.6 41.6 reduce-scatter.5
  336.6 54.4 all-gather.7
  452.8 41.6 reduce-scatter.7
where the time goes:
time: 506 us; the launch traced here: 504 us
  waiting for transfers between devices  290 us (57%)
  local copies, waits for them, and re-layouts  108 us (21%)
  matrix products  82.3 us (16%)
  between operations  13.6 us (3%)
  other arithmetic  10.8 us (2%)
    all_gather x3, waiting for transfers between devices, on_device(): lax.all_gather(current, 'rep', axis=0, tiled=True).reshape(-1, block, C)  164 us
    reduce_scatter x3, waiting for transfers between devices, on_device(): lax.psum_scatter(summed.reshape(lax.axis_size('team') * rows_here, C).ast...  125 us
    gather x24, local copies, waits for them, and re-layouts, on_device(): picked = gathered[columns[:, slot_index]]  96.9 us
    dot_general x24, matrix products, on_device(): jnp.einsum('iab,ibc->iac', panels[:, slot_index], picked, preferred_eleme...  82.3 us
    unnamed x47, local copies, waits for them, and re-layouts  10.7 us
  transfers between devices with their start and end apart: 6, of which 6 were waited for; matrix products, arithmetic and copies ran while one was open for 1% of the time, Pallas kernels for 0%

commit v1 on v0

--- a/solution.py
+++ b/solution.py
@@ -17,7 +17,9 @@
     seeded = (labels[:, None] == classes[None, :]).astype(jnp.float32) * 16.0
     current = seeded.astype(jnp.bfloat16)
     for step_index in range(ITERS):
-        gathered = lax.all_gather(current, "rep", axis=0, tiled=True).reshape(-1, block, C)
+        gathered = jnp.concatenate(
+            lax.all_to_all(jnp.stack([current] * lax.axis_size("rep")), "rep", 0, 0), axis=0
+        ).reshape(-1, block, C)
         block_count = lax.axis_size("team") * rows_here // block
         summed = jnp.zeros((block_count, block, C), jnp.float32)
         for slot_index in range(slots):

time: 506 us -> 514 us (1.016)
  blocking collectives: 0 us -> 116 us
  waiting for transfers between devices: 290 us -> 174 us
  starting transfers between devices: 0.61 us -> 7.29 us
    all_gather x3 -> x0, waiting for transfers between devices: 164 us -> none  [on_device(): lax.all_gather(current, 'rep', axis=0, tiled=True).reshape(-1, block, C)]
    all_to_all x0 -> x2, blocking collectives: none -> 116 us  [on_device(): lax.all_to_all(jnp.stack([current] * lax.axis_size('rep')), 'rep', 0, 0)]
    all_to_all x0 -> x1, waiting for transfers between devices: none -> 47.6 us  [on_device(): lax.all_to_all(jnp.stack([current] * lax.axis_size('rep')), 'rep', 0, 0)]
    all_to_all x0 -> x1, starting transfers between devices: none -> 7.17 us  [on_device(): lax.all_to_all(jnp.stack([current] * lax.axis_size('rep')), 'rep', 0, 0)]
  transfers between devices with their start and end apart: 6 -> 4, of which waited for: 6 -> 4; matrix products, arithmetic and copies ran while one was open for 1% -> 1% of each run, Pallas kernels for 0% -> 0%
where the time goes in v1:
time: 514 us; the launch traced here: 512 us
  waiting for transfers between devices  174 us (34%)
  blocking collectives  116 us (23%)
  local copies, waits for them, and re-layouts  111 us (22%)
  matrix products  82 us (16%)
  between operations  13.3 us (3%)
  other arithmetic  8.66 us (2%)
  starting transfers between devices  7.29 us (1%)
    reduce_scatter x3, waiting for transfers between devices, on_device(): lax.psum_scatter(summed.reshape(lax.axis_size('team') * rows_here, C).ast...  127 us
    all_to_all x2, blocking collectives, on_device(): lax.all_to_all(jnp.stack([current] * lax.axis_size('rep')), 'rep', 0, 0)  116 us
    gather x24, local copies, waits for them, and re-layouts, on_device(): picked = gathered[columns[:, slot_index]]  96.9 us
    dot_general x24, matrix products, on_device(): jnp.einsum('iab,ibc->iac', panels[:, slot_index], picked, preferred_eleme...  82 us
    all_to_all x1, waiting for transfers between devices, on_device(): lax.all_to_all(jnp.stack([current] * lax.axis_size('rep')), 'rep', 0, 0)  47.6 us
    unnamed x47, local copies, waits for them, and re-layouts  10.7 us
  transfers between devices with their start and end apart: 4, of which 4 were waited for; matrix products, arithmetic and copies ran while one was open for 1% of the time, Pallas kernels for 0%

profile of v1, /device:TPU:0, one launch (start us, length us, event | category | flops | bytes accessed | tf_op | source)
XLA Modules:
  0.0 512.4 jit_solution(9077920641586104583)
XLA Ops:
  6.5 0.8 select_convert_fusion
  7.3 2.4 stack.6
  9.7 7.2 %all-to-all-start = ((bf16[16,256,512]{2,1,0:T(8,128)(2,1)}), bf16[16,256,512]{2,1,0:T(8,128)(2,1)}, u32[]{:S(2)}, u32[]{:S(2)}) async-start(bf16[16,256,512]{2,1,0:T(8,128)(2,1)} %stack.6), calls=%async_computation | async-start | bytes 8388608 | tf_op jit(solution)/shard_map/all_to_all | solution.py:21
  16.9 4.7 copy.6
  21.7 47.6 %all-to-all-done = bf16[16,256,512]{2,1,0:T(8,128)(2,1)} async-done(((bf16[16,256,512]{2,1,0:T(8,128)(2,1)}), bf16[16,256,512]{2,1,0:T(8,128)(2,1)}, u32[]{:S(2)}, u32[]{:S(2)}) %all-to-all-start) | async-done | bytes 4194336 | tf_op jit(solution)/shard_map/all_to_all | solution.py:21
  69.3 2.9 gather_fusion.7
  72.2 4.2 gather_fusion.6
  76.4 4.2 gather_fusion.5
  80.6 4.2 gather_fusion.4
  84.8 4.3 gather_fusion.3
  89.0 4.2 gather_fusion.2
  93.2 4.2 gather_fusion.1
  97.4 4.2 gather_fusion
  101.6 2.6 fusion.21
  106.0 0.9 copy-done.13
  106.9 2.7 fusion.15
  109.6 2.7 fusion.12
  112.2 2.6 fusion.9
  114.9 2.6 fusion.6
  117.5 2.7 fusion.3
  120.2 10.8 %add_convert_fusion.2 = bf16[16,512,128]{1,2,0:T(8,128)(2,1)} fusion(f32[16,512,128]{1,2,0:T(8,128)S(1)} %fusion.21, f32[16,512,128]{1,2,0:T(8,128)S(1)} %fusion.18, f32[16,512,128]{1,2,0:T(8,128)} %fusion.15, f32[16,512,128]{1,2,0:T(8,128)} %fusion.12, f32[16,512,128]{1,2,0:T(8,128)} %fusion.9, f32[16,512,128]{1,2,0:T(8,128)} %fusion.3, ...), kind=kOutput, calls=%fused_computation.27 | convolution fusion | flops 276824064 | bytes 34078720 | tf_op jit(solution)/shard_map/iab,ibc->iac/dot_general | solution.py:27
  131.1 51.4 %reduce-scatter.4.cloned.1.call-done = bf16[256,512]{1,0:T(8,128)(2,1)} async-done(((bf16[2048,512]{1,0:T(8,128)(2,1)}), bf16[256,512]{1,0:T(8,128)(2,1)}) %reduce-scatter.4.cloned.1.call-update) | async-done | bytes 262160 | tf_op jit(solution)/shard_map/reduce_scatter | solution.py:30
  182.5 1.2 multiply_reduce_fusion.2
  183.7 1.1 multiply_convert_fusion.2
  185.3 58.2 %all_to_all.15 = bf16[16,256,512]{2,1,0:T(8,128)(2,1)} all-to-all(bf16[16,256,512]{2,1,0:T(8,128)(2,1)S(1)} %stack.7), channel_id=1, replica_groups=mesh['team'=8,'rep'=16] {'rep'}, dimensions={0} | all-to-all | bytes 8388608 | tf_op jit(solution)/shard_map/all_to_all | solution.py:21
  243.5 2.9 gather_fusion.15
  246.4 4.2 gather_fusion.14
  250.5 4.3 gather_fusion.13
  254.8 4.2 gather_fusion.12
  259.0 4.2 gather_fusion.11
  263.2 4.2 gather_fusion.10
  267.4 4.2 gather_fusion.9
  271.6 4.2 gather_fusion.8
  275.8 2.6 fusion.22
  280.1 0.9 copy-done.18
  281.0 2.7 fusion.16
  283.7 2.7 fusion.13
  286.4 2.6 fusion.10
  289.0 2.6 fusion.4
  291.7 2.7 fusion.7
  294.4 10.8 %add_convert_fusion.1 = bf16[16,512,128]{1,2,0:T(8,128)(2,1)} fusion(f32[16,512,128]{1,2,0:T(8,128)S(1)} %fusion.22, f32[16,512,128]{1,2,0:T(8,128)S(1)} %fusion.19, f32[16,512,128]{1,2,0:T(8,128)} %fusion.16, f32[16,512,128]{1,2,0:T(8,128)} %fusion.13, f32[16,512,128]{1,2,0:T(8,128)} %fusion.10, f32[16,512,128]{1,2,0:T(8,128)} %fusion.4, ...), kind=kOutput, calls=%fused_computation.26 | convolution fusion | flops 276824064 | bytes 34078720 | tf_op jit(solution)/shard_map/iab,ibc->iac/dot_general | solution.py:27
  305.2 37.5 %reduce-scatter.6.cloned.1.call-done = bf16[256,512]{1,0:T(8,128)(2,1)} async-done(((bf16[2048,512]{1,0:T(8,128)(2,1)}), bf16[256,512]{1,0:T(8,128)(2,1)}) %reduce-scatter.6.cloned.1.call-update) | async-done | bytes 262160 | tf_op jit(solution)/shard_map/reduce_scatter | solution.py:30
  342.7 1.2 multiply_reduce_fusion.1
  344.0 1.1 multiply_convert_fusion.1
  345.5 58.0 %all_to_all.16 = bf16[16,256,512]{2,1,0:T(8,128)(2,1)} all-to-all(bf16[16,256,512]{2,1,0:T(8,128)(2,1)S(1)} %stack.8), channel_id=1, replica_groups=mesh['team'=8,'rep'=16] {'rep'}, dimensions={0} | all-to-all | bytes 8388608 | tf_op jit(solution)/shard_map/all_to_all | solution.py:21
  403.6 2.9 gather_fusion.23
  406.5 4.2 gather_fusion.22
  410.7 4.2 gather_fusion.21
  414.9 4.2 gather_fusion.20
  419.1 4.3 gather_fusion.19
  423.3 4.2 gather_fusion.18
  427.5 4.2 gather_fusion.17
  431.7 4.2 gather_fusion.16
  435.9 2.6 fusion.5
  440.3 0.9 copy-done.17
  441.2 2.6 fusion.11
  443.8 2.7 fusion.14
  446.5 2.7 fusion.17
  449.2 2.6 fusion.20
  451.8 2.6 fusion.23
  454.4 10.7 %add_convert_fusion = bf16[16,512,128]{1,2,0:T(8,128)(2,1)} fusion(f32[16,512,128]{1,2,0:T(8,128)} %fusion.23, f32[16,512,128]{1,2,0:T(8,128)} %fusion.20, f32[16,512,128]{1,2,0:T(8,128)} %fusion.17, f32[16,512,128]{1,2,0:T(8,128)} %fusion.14, f32[16,512,128]{1,2,0:T(8,128)} %fusion.11, f32[16,512,128]{1,2,0:T(8,128)S(1)} %fusion.5, ...), kind=kOutput, calls=%fused_computation.25 | convolution fusion | flops 276824064 | bytes 34078720 | tf_op jit(solution)/shard_map/iab,ibc->iac/dot_general | solution.py:27
  465.1 37.7 %reduce-scatter.8.cloned.1.call-done = bf16[256,512]{1,0:T(8,128)(2,1)} async-done(((bf16[2048,512]{1,0:T(8,128)(2,1)}), bf16[256,512]{1,0:T(8,128)(2,1)}) %reduce-scatter.8.cloned.1.call-update) | async-done | bytes 262160 | tf_op jit(solution)/shard_map/reduce_scatter | solution.py:30
  502.8 1.2 multiply_reduce_fusion
  504.1 1.9 multiply_convert_fusion
  (62 shorter events, 6.3 us)
Async XLA Ops:
  9.7 59.6 %all-to-all-start = ((bf16[16,256,512]{2,1,0:T(8,128)(2,1)}), bf16[16,256,512]{2,1,0:T(8,128)(2,1)}, u32[]{:S(2)}, u32[]{:S(2)}) async-start(bf16[16,256,512]{2,1,0:T(8,128)(2,1)} %stack.6), calls=%async_computation | async-start | bytes 8388608 | tf_op jit(solution)/shard_map/all_to_all | solution.py:21
  16.9 4.8 copy-start.22
  16.9 165.6 %reduce-scatter.4.cloned.1.call-start = ((), (), s32[]{:S(2)}) async-start(), calls=%async_computation.6 | async-start | bytes 2359296 | tf_op jit(solution)/shard_map/reduce_scatter | solution.py:30
  101.6 3.0 copy-start
  101.6 3.7 copy-start.12
  105.3 1.6 copy-start.13
  106.9 2.7 copy-start.10
  109.6 2.7 copy-start.11
  112.2 2.6 copy-start.8
  114.9 2.6 copy-start.9
  131.0 51.5 %copy-start.21 = (s32[256]{0:T(256)S(1)}, s32[256]{0:T(256)}, u32[]{:S(2)}) copy-start(s32[256]{0:T(256)} %param.5) | copy-start | bytes 3076
  131.0 211.7 %reduce-scatter.6.cloned.1.call-start = ((), (), s32[]{:S(2)}) async-start(), calls=%async_computation.7 | async-start | bytes 2359296 | tf_op jit(solution)/shard_map/reduce_scatter | solution.py:30
  275.8 3.0 copy-start.1
  275.8 3.7 copy-start.19
  279.4 1.6 copy-start.18
  281.0 2.7 copy-start.16
  283.7 2.7 copy-start.14
  286.4 2.6 copy-start.15
  289.0 2.6 copy-start.6
  305.2 197.6 %reduce-scatter.8.cloned.1.call-start = ((), (), s32[]{:S(2)}) async-start(), calls=%async_computation.8 | async-start | bytes 2359296 | tf_op jit(solution)/shard_map/reduce_scatter | solution.py:30
  435.9 3.0 copy-start.2
  435.9 3.7 copy-start.20
  439.6 1.6 copy-start.17
  441.2 2.6 copy-start.7
  443.8 2.7 copy-start.5
  446.5 2.7 copy-start.4
  449.2 2.6 copy-start.3
Sparse Core Ops, SparseCore 0:
  131.1 51.2 reduce-scatter.3
  305.3 37.3 reduce-scatter.5
  465.2 37.5 reduce-scatter.7
